TPU v7x, 32 devices: a whole 2x2x4 slice. The times are simulated.
32 devices in a mesh: grp: 2 (over y), sec: 4 (over z), col: 2 (over x), rep: 2 (over core).
Axes of the slice: x: 2, y: 2, z: 4, core: 2. Of those that a mesh axis runs over, the one named last changes fastest.
Arguments:
- corners: bfloat16 [4, 2, 4, 128, 128], P(('grp', 'col'), None, 'sec', 'rep'), parts along dimension 0, may hold values from -6 to 6
- edges: bfloat16 [4, 2, 4, 128, 6272], P(('grp', 'col'), None, 'sec'), parts along dimension 0, may hold values from -0.5 to 0.5
- projectors: bfloat16 [4, 2, 4, 128, 6272], P(('grp', 'col'), None, 'sec', 'rep'), parts along dimension 0, may hold values from -0.078125 to 0.078125
- sector_sizes: int32 [4], replicated, may hold values from 1 to 128, 192 in all
Outputs:
- new_corners: bfloat16 [4, 2, 4, 128, 128], P(('grp', 'col'), None, 'sec', 'rep'), parts along dimension 0
- log_scales: float32 [4, 2, 4], P(('grp', 'col')), parts along dimension 0
There are 2 independent parts, one for each index of `grp`. A program takes and returns all parts, laid end to end along the dimension named above; an argument that names none is the same for every part. Nothing has to cross between parts.
Inputs may be any that keep to these rules, and one draw needn't show every extreme that they name: `sector_sizes`: sector sizes sum to 192; the largest is exactly 128.
All inputs are finite; a program needn't handle non-finite values.
Results may differ from a plain program's by a relative error of at most 0.013.
Values may be sent and summed in bfloat16 or wider, within the bound.
A program may use at most 64 MiB of HBM per device.

v0:
```python
import jax
import jax.numpy as jnp
from jax import lax
from jax.sharding import PartitionSpec as P

K_NEG = 16
K_ZERO = 17
ITERS = 4


def with_halo(block, sides, width):
    for axis, dim in sides:
        count = lax.axis_size(axis)
        forward = [(i, i + 1) for i in range(count - 1)]
        backward = [(target, source) for source, target in forward]
        low = lax.ppermute(
            lax.slice_in_dim(block, block.shape[dim] - width, None, axis=dim), axis, forward
        )
        high = lax.ppermute(lax.slice_in_dim(block, 0, width, axis=dim), axis, backward)
        block = jnp.concatenate([low, block, high], axis=dim)
    return block


def shifted(array, axis, by):
    peers = lax.axis_size(axis)
    return lax.ppermute(array, axis, [(i, (i + by) % peers) for i in range(peers)])


def project(proj_part, block_part, half, block):
    shaped = block_part.reshape(2, half, -1, block)
    return jnp.einsum("rakp,rakb->rpb", proj_part, shaped, preferred_element_type=jnp.float32)


def on_device(corners, edges, projectors, sector_sizes):
    half = corners.shape[3]
    block = corners.shape[4]
    width = edges.shape[4]
    states = width // block
    sector = lax.axis_index("sec")
    row_half = lax.axis_index("rep")
    live = jnp.sum(jnp.where(jnp.arange(sector_sizes.shape[0]) == sector, sector_sizes, 0))
    row_ids = row_half * half + jnp.arange(half)
    col_ids = jnp.arange(block)
    keep = (row_ids[:, None] < live) & (col_ids[None, :] < live)
    count = jnp.sum(sector_sizes.astype(jnp.float32) ** 2)
    current = jnp.where(keep[None], corners[0, :, 0], jnp.zeros_like(corners[0, :, 0]))
    edge = edges[0, :, 0]
    proj = projectors[0, :, 0].reshape(2, half, states, block)
    rise = K_NEG + K_ZERO
    logs = []
    for step in range(ITERS):
        absorbed = jnp.einsum(
            "rax,rxn->ran", current, edge, preferred_element_type=jnp.float32
        ).astype(jnp.bfloat16)
        padded = with_halo(absorbed[:, None], (("sec", 1),), 1)
        from_lower = padded[:, 0, :, rise * block :]
        own_part = padded[:, 1, :, K_NEG * block : rise * block]
        from_upper = padded[:, 2, :, : K_NEG * block]
        partial_value = project(proj[:, :, rise:], from_lower, half, block)
        partial_value = partial_value + project(proj[:, :, K_NEG:rise], own_part, half, block)
        partial_value = partial_value + project(proj[:, :, :K_NEG], from_upper, half, block)
        summed = lax.psum_scatter(partial_value, "rep", scatter_dimension=1, tiled=True)
        masked = jnp.where(keep[None], summed, jnp.float32(0.0))
        scale = lax.psum(jnp.sum(masked * masked, axis=(1, 2)), ("sec", "rep"))
        factor = scale / count + 1e-06
        logs.append(jnp.log(factor))
        fresh = (masked / jnp.sqrt(factor)[:, None, None]).astype(jnp.bfloat16)
        current = shifted(fresh, "col", 1)
    return (current[None, :, None], jnp.stack(logs, axis=-1)[None])


def solution(mesh):
    in_specs = (
        P(("grp", "col"), None, "sec", "rep", None),
        P(("grp", "col"), None, "sec", None, None),
        P(("grp", "col"), None, "sec", "rep", None),
        P(),
    )
    out_specs = (P(("grp", "col"), None, "sec", "rep", None), P(("grp", "col"), None, None))
    return jax.shard_map(
        on_device, mesh=mesh, in_specs=in_specs, out_specs=out_specs, check_vma=False
    )
```

profile of v0, /device:TPU:0, one launch (start us, length us, event | category | flops | bytes accessed | tf_op | source)
XLA Modules:
  0.0 357.4 jit_solution(14551828280000541907)
XLA Ops:
  7.2 1.4 fusion.46
  10.1 2.5 fusion
  12.6 1.3 collective-permute-start.1
  13.9 6.7 %collective-permute-start = (bf16[2,1,64,6272]{3,2,0,1:T(8,128)(2,1)}, bf16[2,1,64,6272]{3,2,0,1:T(8,128)(2,1)}, u32[]{:S(2)}, u32[]{:S(2)}) collective-permute-start(bf16[2,1,64,6272]{3,2,0,1:T(8,128)(2,1)} %fusion), channel_id=1, source_target_pairs={{0,4},{4,8},{8,12},{1,5},{5,9},{9,13},{2,6},{6,10},{10,14},{3,7},{... | collective-permute-start | bytes 4816904 | tf_op jit(solution)/shard_map/ppermute | solution.py:16
  20.6 1.9 slice.71
  22.5 3.9 %reshape_squeeze.40 = bf16[2,64,49,128]{3,2,1,0:T(8,128)(2,1)} reshape(bf16[1,2,1,64,6272]{4,3,2,1,0:T(8,128)(2,1)} %param.6) | data formatting | bytes 3211264 | tf_op jit(solution)/shard_map/reshape;squeeze | solution.py:48
  26.4 2.1 reshape_squeeze.41
  28.5 1.2 slice.72
  29.8 1.8 convolution_bitcast_fusion.10
  31.6 21.3 %collective-permute-done.1 = bf16[2,1,64,6272]{3,2,0,1:T(8,128)(2,1)} collective-permute-done((bf16[2,1,64,6272]{3,2,0,1:T(8,128)(2,1)}, bf16[2,1,64,6272]{3,2,0,1:T(8,128)(2,1)}, u32[]{:S(2)}, u32[]{:S(2)}) %collective-permute-start.1) | collective-permute-done | bytes 1605664 | tf_op jit(solution)/shard_map/ppermute | solution.py:19
  54.5 1.1 slice.69
  58.2 19.9 %all-reduce.9.cloned.1.call-done = f32[2,128,128]{2,0,1:T(2,128)} async-done(((f32[2,128,128]{2,0,1:T(2,128)}), f32[2,128,128]{2,0,1:T(2,128)}) %all-reduce.9.cloned.1.call-update) | async-done | bytes 131088
  79.6 17.1 %psum.28 = f32[2]{0:T(128)S(1)} all-reduce(f32[2]{0:T(128)S(1)} %multiply_reduce_fusion.3), channel_id=1, replica_groups=mesh['grp'=2,'sec'=4,'col'=2,'rep'=2] {'sec','rep'}, use_global_device_ids=true, to_apply=%region_3.4 | all-reduce | flops 2 | bytes 16 | tf_op jit(solution)/shard_map/psum | solution.py:64
  97.4 1.5 collective-permute-start.2
  99.0 2.4 collective-permute-done.2
  101.4 1.7 fusion.1
  103.2 1.3 collective-permute-start.4
  104.4 5.7 %collective-permute-start.3 = (bf16[2,1,64,6272]{3,2,0,1:T(8,128)(2,1)}, bf16[2,1,64,6272]{3,2,0,1:T(8,128)(2,1)}, u32[]{:S(2)}, u32[]{:S(2)}) collective-permute-start(bf16[2,1,64,6272]{3,2,0,1:T(8,128)(2,1)} %fusion.1), channel_id=1, source_target_pairs={{0,4},{4,8},{8,12},{1,5},{5,9},{9,13},{2,6},{6,10},{10,14},{3,7},{... | collective-permute-start | bytes 4816904 | tf_op jit(solution)/shard_map/ppermute | solution.py:16
  110.2 2.0 slice.76
  112.1 2.1 reshape_squeeze.44
  114.3 1.9 convolution_bitcast_fusion.7
  116.2 21.6 %collective-permute-done.4 = bf16[2,1,64,6272]{3,2,0,1:T(8,128)(2,1)} collective-permute-done((bf16[2,1,64,6272]{3,2,0,1:T(8,128)(2,1)}, bf16[2,1,64,6272]{3,2,0,1:T(8,128)(2,1)}, u32[]{:S(2)}, u32[]{:S(2)}) %collective-permute-start.4) | collective-permute-done | bytes 1605664 | tf_op jit(solution)/shard_map/ppermute | solution.py:19
  141.8 19.8 %all-reduce.11.cloned.1.call-done = f32[2,128,128]{2,0,1:T(2,128)} async-done(((f32[2,128,128]{2,0,1:T(2,128)}), f32[2,128,128]{2,0,1:T(2,128)}) %all-reduce.11.cloned.1.call-update) | async-done | bytes 131088
  162.6 17.1 %psum.29 = f32[2]{0:T(128)S(1)} all-reduce(f32[2]{0:T(128)S(1)} %multiply_reduce_fusion.2), channel_id=1, replica_groups=mesh['grp'=2,'sec'=4,'col'=2,'rep'=2] {'sec','rep'}, use_global_device_ids=true, to_apply=%region_7.8 | all-reduce | flops 2 | bytes 16 | tf_op jit(solution)/shard_map/psum | solution.py:64
  180.4 1.5 collective-permute-start.5
  181.9 2.4 collective-permute-done.5
  184.4 1.7 fusion.2
  186.1 1.3 collective-permute-start.7
  187.4 5.7 %collective-permute-start.6 = (bf16[2,1,64,6272]{3,2,0,1:T(8,128)(2,1)}, bf16[2,1,64,6272]{3,2,0,1:T(8,128)(2,1)}, u32[]{:S(2)}, u32[]{:S(2)}) collective-permute-start(bf16[2,1,64,6272]{3,2,0,1:T(8,128)(2,1)} %fusion.2), channel_id=1, source_target_pairs={{0,4},{4,8},{8,12},{1,5},{5,9},{9,13},{2,6},{6,10},{10,14},{3,7},{... | collective-permute-start | bytes 4816904 | tf_op jit(solution)/shard_map/ppermute | solution.py:16
  193.1 2.0 slice.79
  195.1 2.1 reshape_squeeze.47
  197.2 1.9 convolution_bitcast_fusion.4
  199.1 21.6 %collective-permute-done.7 = bf16[2,1,64,6272]{3,2,0,1:T(8,128)(2,1)} collective-permute-done((bf16[2,1,64,6272]{3,2,0,1:T(8,128)(2,1)}, bf16[2,1,64,6272]{3,2,0,1:T(8,128)(2,1)}, u32[]{:S(2)}, u32[]{:S(2)}) %collective-permute-start.7) | collective-permute-done | bytes 1605664 | tf_op jit(solution)/shard_map/ppermute | solution.py:19
  224.7 19.8 %all-reduce.13.cloned.1.call-done = f32[2,128,128]{2,0,1:T(2,128)} async-done(((f32[2,128,128]{2,0,1:T(2,128)}), f32[2,128,128]{2,0,1:T(2,128)}) %all-reduce.13.cloned.1.call-update) | async-done | bytes 131088
  245.5 17.1 %psum.30 = f32[2]{0:T(128)S(1)} all-reduce(f32[2]{0:T(128)S(1)} %multiply_reduce_fusion.1), channel_id=1, replica_groups=mesh['grp'=2,'sec'=4,'col'=2,'rep'=2] {'sec','rep'}, use_global_device_ids=true, to_apply=%region_10.11 | all-reduce | flops 2 | bytes 16 | tf_op jit(solution)/shard_map/psum | solution.py:64
  263.3 1.5 collective-permute-start.8
  264.9 2.4 collective-permute-done.8
  267.3 1.7 fusion.3
  269.1 1.3 collective-permute-start.10
  270.3 5.7 %collective-permute-start.9 = (bf16[2,1,64,6272]{3,2,0,1:T(8,128)(2,1)}, bf16[2,1,64,6272]{3,2,0,1:T(8,128)(2,1)}, u32[]{:S(2)}, u32[]{:S(2)}) collective-permute-start(bf16[2,1,64,6272]{3,2,0,1:T(8,128)(2,1)} %fusion.3), channel_id=1, source_target_pairs={{0,4},{4,8},{8,12},{1,5},{5,9},{9,13},{2,6},{6,10},{10,14},{3,7},{... | collective-permute-start | bytes 4816904 | tf_op jit(solution)/shard_map/ppermute | solution.py:16
  276.1 2.0 slice.82
  278.0 2.1 reshape_squeeze.50
  280.2 1.9 convolution_bitcast_fusion.1
  282.1 21.6 %collective-permute-done.10 = bf16[2,1,64,6272]{3,2,0,1:T(8,128)(2,1)} collective-permute-done((bf16[2,1,64,6272]{3,2,0,1:T(8,128)(2,1)}, bf16[2,1,64,6272]{3,2,0,1:T(8,128)(2,1)}, u32[]{:S(2)}, u32[]{:S(2)}) %collective-permute-start.10) | collective-permute-done | bytes 1605664 | tf_op jit(solution)/shard_map/ppermute | solution.py:19
  307.6 19.9 %all-reduce.15.cloned.1.call-done = f32[2,128,128]{2,0,1:T(2,128)} async-done(((f32[2,128,128]{2,0,1:T(2,128)}), f32[2,128,128]{2,0,1:T(2,128)}) %all-reduce.15.cloned.1.call-update) | async-done | bytes 131088
  328.5 17.1 %psum.31 = f32[2]{0:T(128)S(1)} all-reduce(f32[2]{0:T(128)S(1)} %multiply_reduce_fusion), channel_id=1, replica_groups=mesh['grp'=2,'sec'=4,'col'=2,'rep'=2] {'sec','rep'}, use_global_device_ids=true, to_apply=%region_13.14 | all-reduce | flops 2 | bytes 16 | tf_op jit(solution)/shard_map/psum | solution.py:64
  346.3 1.5 collective-permute-start.11
  348.5 1.8 collective-permute-done.11
  (83 shorter events, 25.4 us)
Async XLA Ops:
  7.2 2.9 copy-start
  7.2 70.9 %all-reduce.9.cloned.1.call-start = ((), (), s32[]{:S(2)}) async-start(), calls=%async_computation | async-start | bytes 262144
  12.6 40.3 %collective-permute-start.1 = (bf16[2,1,64,6272]{3,2,0,1:T(8,128)(2,1)}, bf16[2,1,64,6272]{3,2,0,1:T(8,128)(2,1)}, u32[]{:S(2)}, u32[]{:S(2)}) collective-permute-start(bf16[2,1,64,6272]{3,2,0,1:T(8,128)(2,1)} %fusion), channel_id=1, source_target_pairs={{4,0},{8,4},{12,8},{5,1},{9,5},{13,9},{6,2},{10,6},{14,10},{7,3},{... | collective-permute-start | bytes 4816904 | tf_op jit(solution)/shard_map/ppermute | solution.py:19
  13.9 40.6 %collective-permute-start = (bf16[2,1,64,6272]{3,2,0,1:T(8,128)(2,1)}, bf16[2,1,64,6272]{3,2,0,1:T(8,128)(2,1)}, u32[]{:S(2)}, u32[]{:S(2)}) collective-permute-start(bf16[2,1,64,6272]{3,2,0,1:T(8,128)(2,1)} %fusion), channel_id=1, source_target_pairs={{0,4},{4,8},{8,12},{1,5},{5,9},{9,13},{2,6},{6,10},{10,14},{3,7},{... | collective-permute-start | bytes 4816904 | tf_op jit(solution)/shard_map/ppermute | solution.py:16
  29.8 24.3 %copy-start.5 = (bf16[2,64,17,128]{3,2,1,0:T(8,128)(2,1)}, bf16[2,64,17,128]{3,2,1,0:T(8,128)(2,1)S(1)}, u32[]{:S(2)}) copy-start(bf16[2,64,17,128]{3,2,1,0:T(8,128)(2,1)S(1)} %slice.72) | copy-start | bytes 1671172
  29.8 24.3 %copy-start.1 = (bf16[2,64,49,128]{3,2,1,0:T(8,128)(2,1)S(1)}, bf16[2,64,49,128]{3,2,1,0:T(8,128)(2,1)}, u32[]{:S(2)}) copy-start(bf16[2,64,49,128]{3,2,1,0:T(8,128)(2,1)} %reshape_squeeze.40) | copy-start | bytes 4816900
  55.7 1.3 copy-start.7
  55.7 23.3 %copy-start.6 = (s32[4]{0:T(128)S(1)}, s32[4]{0:T(128)}, u32[]{:S(2)}) copy-start(s32[4]{0:T(128)} %param.7) | copy-start | bytes 52
  56.9 104.7 %all-reduce.11.cloned.1.call-start = ((), (), s32[]{:S(2)}) async-start(), calls=%async_computation.1 | async-start | bytes 262144
  97.4 4.0 %collective-permute-start.2 = (bf16[2,64,128]{2,1,0:T(8,128)(2,1)S(1)}, bf16[2,64,128]{2,1,0:T(8,128)(2,1)S(1)}, u32[]{:S(2)}, u32[]{:S(2)}) collective-permute-start(bf16[2,64,128]{2,1,0:T(8,128)(2,1)S(1)} %divide_convert_fusion.3), channel_id=1, source_target_pairs={{0,2},{2,0},{1,3},{3,1},{4,6},{6,4},{5,7},{7,5},{8,10},{10,8},{9,1... | collective-permute-start | bytes 98312 | tf_op jit(solution)/shard_map/ppermute | solution.py:26
  103.2 34.6 %collective-permute-start.4 = (bf16[2,1,64,6272]{3,2,0,1:T(8,128)(2,1)}, bf16[2,1,64,6272]{3,2,0,1:T(8,128)(2,1)}, u32[]{:S(2)}, u32[]{:S(2)}) collective-permute-start(bf16[2,1,64,6272]{3,2,0,1:T(8,128)(2,1)} %fusion.1), channel_id=1, source_target_pairs={{4,0},{8,4},{12,8},{5,1},{9,5},{13,9},{6,2},{10,6},{14,10},{7,3},{... | collective-permute-start | bytes 4816904 | tf_op jit(solution)/shard_map/ppermute | solution.py:19
  104.4 34.9 %collective-permute-start.3 = (bf16[2,1,64,6272]{3,2,0,1:T(8,128)(2,1)}, bf16[2,1,64,6272]{3,2,0,1:T(8,128)(2,1)}, u32[]{:S(2)}, u32[]{:S(2)}) collective-permute-start(bf16[2,1,64,6272]{3,2,0,1:T(8,128)(2,1)} %fusion.1), channel_id=1, source_target_pairs={{0,4},{4,8},{8,12},{1,5},{5,9},{9,13},{2,6},{6,10},{10,14},{3,7},{... | collective-permute-start | bytes 4816904 | tf_op jit(solution)/shard_map/ppermute | solution.py:16
  114.3 24.7 %copy-start.2 = (bf16[2,64,49,128]{3,2,1,0:T(8,128)(2,1)S(1)}, bf16[2,64,49,128]{3,2,1,0:T(8,128)(2,1)}, u32[]{:S(2)}) copy-start(bf16[2,64,49,128]{3,2,1,0:T(8,128)(2,1)} %reshape_squeeze.40) | copy-start | bytes 4816900
  141.7 102.8 %all-reduce.13.cloned.1.call-start = ((), (), s32[]{:S(2)}) async-start(), calls=%async_computation.2 | async-start | bytes 262144
  180.4 4.0 %collective-permute-start.5 = (bf16[2,64,128]{2,1,0:T(8,128)(2,1)S(1)}, bf16[2,64,128]{2,1,0:T(8,128)(2,1)S(1)}, u32[]{:S(2)}, u32[]{:S(2)}) collective-permute-start(bf16[2,64,128]{2,1,0:T(8,128)(2,1)S(1)} %divide_convert_fusion.2), channel_id=1, source_target_pairs={{0,2},{2,0},{1,3},{3,1},{4,6},{6,4},{5,7},{7,5},{8,10},{10,8},{9,1... | collective-permute-start | bytes 98312 | tf_op jit(solution)/shard_map/ppermute | solution.py:26
  186.1 34.6 %collective-permute-start.7 = (bf16[2,1,64,6272]{3,2,0,1:T(8,128)(2,1)}, bf16[2,1,64,6272]{3,2,0,1:T(8,128)(2,1)}, u32[]{:S(2)}, u32[]{:S(2)}) collective-permute-start(bf16[2,1,64,6272]{3,2,0,1:T(8,128)(2,1)} %fusion.2), channel_id=1, source_target_pairs={{4,0},{8,4},{12,8},{5,1},{9,5},{13,9},{6,2},{10,6},{14,10},{7,3},{... | collective-permute-start | bytes 4816904 | tf_op jit(solution)/shard_map/ppermute | solution.py:19
  187.4 34.9 %collective-permute-start.6 = (bf16[2,1,64,6272]{3,2,0,1:T(8,128)(2,1)}, bf16[2,1,64,6272]{3,2,0,1:T(8,128)(2,1)}, u32[]{:S(2)}, u32[]{:S(2)}) collective-permute-start(bf16[2,1,64,6272]{3,2,0,1:T(8,128)(2,1)} %fusion.2), channel_id=1, source_target_pairs={{0,4},{4,8},{8,12},{1,5},{5,9},{9,13},{2,6},{6,10},{10,14},{3,7},{... | collective-permute-start | bytes 4816904 | tf_op jit(solution)/shard_map/ppermute | solution.py:16
  197.2 24.7 %copy-start.3 = (bf16[2,64,49,128]{3,2,1,0:T(8,128)(2,1)S(1)}, bf16[2,64,49,128]{3,2,1,0:T(8,128)(2,1)}, u32[]{:S(2)}) copy-start(bf16[2,64,49,128]{3,2,1,0:T(8,128)(2,1)} %reshape_squeeze.40) | copy-start | bytes 4816900
  224.7 102.8 %all-reduce.15.cloned.1.call-start = ((), (), s32[]{:S(2)}) async-start(), calls=%async_computation.3 | async-start | bytes 262144
  263.3 4.0 %collective-permute-start.8 = (bf16[2,64,128]{2,1,0:T(8,128)(2,1)S(1)}, bf16[2,64,128]{2,1,0:T(8,128)(2,1)S(1)}, u32[]{:S(2)}, u32[]{:S(2)}) collective-permute-start(bf16[2,64,128]{2,1,0:T(8,128)(2,1)S(1)} %divide_convert_fusion.1), channel_id=1, source_target_pairs={{0,2},{2,0},{1,3},{3,1},{4,6},{6,4},{5,7},{7,5},{8,10},{10,8},{9,1... | collective-permute-start | bytes 98312 | tf_op jit(solution)/shard_map/ppermute | solution.py:26
  269.1 34.6 %collective-permute-start.10 = (bf16[2,1,64,6272]{3,2,0,1:T(8,128)(2,1)}, bf16[2,1,64,6272]{3,2,0,1:T(8,128)(2,1)}, u32[]{:S(2)}, u32[]{:S(2)}) collective-permute-start(bf16[2,1,64,6272]{3,2,0,1:T(8,128)(2,1)} %fusion.3), channel_id=1, source_target_pairs={{4,0},{8,4},{12,8},{5,1},{9,5},{13,9},{6,2},{10,6},{14,10},{7,3},{... | collective-permute-start | bytes 4816904 | tf_op jit(solution)/shard_map/ppermute | solution.py:19
  270.3 34.9 %collective-permute-start.9 = (bf16[2,1,64,6272]{3,2,0,1:T(8,128)(2,1)}, bf16[2,1,64,6272]{3,2,0,1:T(8,128)(2,1)}, u32[]{:S(2)}, u32[]{:S(2)}) collective-permute-start(bf16[2,1,64,6272]{3,2,0,1:T(8,128)(2,1)} %fusion.3), channel_id=1, source_target_pairs={{0,4},{4,8},{8,12},{1,5},{5,9},{9,13},{2,6},{6,10},{10,14},{3,7},{... | collective-permute-start | bytes 4816904 | tf_op jit(solution)/shard_map/ppermute | solution.py:16
  280.2 24.7 %copy-start.4 = (bf16[2,64,49,128]{3,2,1,0:T(8,128)(2,1)S(1)}, bf16[2,64,49,128]{3,2,1,0:T(8,128)(2,1)}, u32[]{:S(2)}) copy-start(bf16[2,64,49,128]{3,2,1,0:T(8,128)(2,1)} %reshape_squeeze.40) | copy-start | bytes 4816900
  346.3 4.0 %collective-permute-start.11 = (bf16[2,64,128]{2,1,0:T(8,128)(2,1)S(1)}, bf16[2,64,128]{2,1,0:T(8,128)(2,1)S(1)}, u32[]{:S(2)}, u32[]{:S(2)}) collective-permute-start(bf16[2,64,128]{2,1,0:T(8,128)(2,1)S(1)} %divide_convert_fusion), channel_id=1, source_target_pairs={{0,2},{2,0},{1,3},{3,1},{4,6},{6,4},{5,7},{7,5},{8,10},{10,8},{9,1... | collective-permute-start | bytes 98312 | tf_op jit(solution)/shard_map/ppermute | solution.py:26
Sparse Core Ops, SparseCore 0:
  57.0 21.0 all-reduce.8
  141.9 19.7 all-reduce.10
  224.8 19.7 all-reduce.12
  307.7 19.7 all-reduce.14
where the time goes:
time: 359 us; the launch traced here: 357 us
  waiting for transfers between devices  175 us (49%)
  blocking collectives  68.2 us (19%)
  local copies, waits for them, and re-layouts  39.3 us (11%)
  starting transfers between devices  35.3 us (10%)
  matrix products  18.2 us (5%)
  between operations  14.8 us (4%)
  other arithmetic  6.8 us (2%)
    ppermute x4, waiting for transfers between devices, with_halo(): lax.ppermute(lax.slice_in_dim(block, 0, width, axis=dim), axis, backward)  86.1 us
    unnamed x8, waiting for transfers between devices  79.5 us
    psum x4, blocking collectives, on_device(): scale = lax.psum(jnp.sum(masked * masked, axis=(1, 2)), ('sec', 'rep'))  68.2 us
    ppermute x4, starting transfers between devices, with_halo(): lax.ppermute(lax.slice_in_dim(block, block.shape[dim] - width, None, axis...  23.9 us
    dot_general x12, matrix products, project(): jnp.einsum('rakp,rakb->rpb', proj_part, shaped, preferred_element_type=jn...  10.5 us
    ppermute x4, waiting for transfers between devices, shifted(): lax.ppermute(array, axis, [(i, (i + by) % peers) for i in range(peers)])  9.12 us
    another operation x4, local copies, waits for them, and re-layouts, project(): shaped = block_part.reshape(2, half, -1, block)  8.58 us
    slice x4, local copies, waits for them, and re-layouts, on_device(): own_part = padded[:, 1, :, K_NEG * block:rise * block]  7.76 us
  transfers between devices with their start and end apart: 16, of which 12 were waited for; matrix products, arithmetic and copies ran while one was open for 10% of the time, Pallas kernels for 0%

commit v1 on v0

v1 whole, which is shorter than its diff:
```python
import functools

import jax
import jax.numpy as jnp
from jax import lax
from jax.experimental import pallas as pl
from jax.experimental.pallas import tpu as pltpu
from jax.sharding import PartitionSpec as P

K_NEG = 16
K_ZERO = 17
ITERS = 4
MESH = pl.DeviceIdType.MESH
F32 = jnp.float32
BF16 = jnp.bfloat16


def rolled(x, axis):
    half = x.shape[axis] // 2
    lo = lax.slice_in_dim(x, 0, half, axis=axis)
    hi = lax.slice_in_dim(x, half, 2 * half, axis=axis)
    return jnp.concatenate([hi, lo], axis=axis)


def kernel(
    ncol, nsec, block, states, narrow,
    sizes, corners, edges, projectors,
    out, logs,
    own, stage, packed, halo, proj, projt, first, cur, sent, scale, tiles, fin, last, all_last, last_tile,
    load_sem, halo_send, halo_recv, proj_send, proj_recv, first_send, first_recv,
    cur_send, cur_recv, scale_send, scale_recv, fin_send, fin_recv, next_send, next_recv, log_send, log_recv,
):
    half = block // 2
    rise = K_NEG + K_ZERO
    wide = K_NEG * block // 2
    c, t, r = lax.axis_index("col"), lax.axis_index("sec"), lax.axis_index("rep")
    other = 1 - r
    right = lax.rem(c + 1, ncol)
    pair = 2 * nsec
    me = t * 2 + r

    load_own = pltpu.make_async_copy(
        edges.at[r, :, K_NEG * block : rise * block], own, load_sem.at[0]
    )
    load_proj = pltpu.make_async_copy(projectors.at[r], proj.at[r], load_sem.at[1])
    loads = []
    if narrow:
        loads = [
            pltpu.make_async_copy(edges.at[r, :, rise * block :], stage.at[0], load_sem.at[2]),
            pltpu.make_async_copy(edges.at[r, :, : K_NEG * block], stage.at[1], load_sem.at[3]),
        ]
    for copy in loads + [load_proj, load_own]:
        copy.start()

    barrier = pltpu.get_barrier_semaphore()
    everyone = ncol * pair
    spot = c * pair + me

    @pl.loop(1, everyone)
    def _(step):
        to = lax.rem(spot + step, everyone)
        pl.semaphore_signal(
            barrier, inc=1,
            device_id={"col": to // pair, "sec": lax.rem(to, pair) // 2, "rep": lax.rem(to, 2)},
            device_id_type=MESH,
        )

    live = sizes[t]
    count = jnp.float32(0.0)
    for s in range(nsec):
        size = sizes[s].astype(F32)
        count = count + size * size
    rows = lax.broadcasted_iota(jnp.int32, (block, block), 0)
    lanes = lax.broadcasted_iota(jnp.int32, (block, block), 1)
    keep = (rows < live) & (lanes < live)
    half_rows = lax.broadcasted_iota(jnp.int32, (half, block), 0) + r * half
    half_lanes = lax.broadcasted_iota(jnp.int32, (half, block), 1)
    half_keep = (half_rows < live) & (half_lanes < live)
    for which in range(2):
        value = corners[which].astype(F32)
        first[which] = jnp.where(half_keep, value, 0.0).astype(BF16)

    @pl.when(t == 0)
    def _():
        cur[:, 0] = jnp.zeros((ITERS, 2, half, block), BF16)
        halo[0] = jnp.zeros((2, block, wide), BF16)

    @pl.when(t == nsec - 1)
    def _():
        cur[:, 2] = jnp.zeros((ITERS, 2, half, block), BF16)
        halo[1] = jnp.zeros((2, block, wide), BF16)

    pl.semaphore_wait(barrier, everyone - 1)

    has_low, has_high = t > 0, t < nsec - 1

    def guarded(dt, action):
        if dt == 0:
            action()
        else:
            pl.when(has_high if dt > 0 else has_low)(action)

    send_proj = pltpu.make_async_remote_copy(
        src_ref=projectors.at[other], dst_ref=proj.at[r],
        send_sem=proj_send, recv_sem=proj_recv,
        device_id={"rep": other}, device_id_type=MESH,
    )
    send_proj.start()

    def first_copy(dt, which):
        side = r if which == 0 else other
        return pltpu.make_async_remote_copy(
            src_ref=first.at[side], dst_ref=cur.at[0, 1 - dt, r],
            send_sem=first_send.at[dt + 1, which], recv_sem=first_recv.at[1 - dt, which],
            device_id={"sec": t + dt, "rep": side}, device_id_type=MESH,
        )

    firsts = [(0, 1), (1, 0), (1, 1), (-1, 0), (-1, 1)]
    for dt, which in firsts:
        guarded(dt, lambda dt=dt, which=which: first_copy(dt, which).start())
    cur[0, 1, r] = first[r]

    def halo_copy(side, part):
        if narrow:
            src = packed.at[side]
        else:
            start = (rise * block if side == 0 else 0) + part * wide
            src = edges.at[r, :, start : start + wide]
        return pltpu.make_async_remote_copy(
            src_ref=src, dst_ref=halo.at[side, part],
            send_sem=halo_send.at[side, part], recv_sem=halo_recv.at[side, part],
            device_id={"sec": t + 1 - 2 * side}, device_id_type=MESH,
        )

    parts = 1 if narrow else 2
    for side in range(2):
        if narrow:
            loads[side].wait()
            for j in range(K_NEG // 2):
                low = stage[side, :, j * block : (j + 1) * block]
                high = stage[side, :, wide + j * block : wide + (j + 1) * block]
                by_row = jnp.concatenate([low[:half], high[:half]], axis=0)
                by_lane = jnp.concatenate([low[:, :half], high[:, :half]], axis=1)
                mixed = jnp.where(live > half, by_lane.astype(F32), by_row.astype(F32))
                packed[side, :, j * block : (j + 1) * block] = mixed.astype(BF16)

        def go(side=side):
            for part in range(parts):
                halo_copy(side, part).start()

        guarded(1 - 2 * side, go)

    load_proj.wait()
    send_proj.wait_recv()
    for k in range(states):
        piece = proj[:, :, k * block : (k + 1) * block].reshape(block, block)
        projt[:, k * block : (k + 1) * block] = piece.T
    load_own.wait()

    def part_of(corner, edge, start):
        number = edge.shape[1] // block
        absorbed = jnp.dot(corner, edge, preferred_element_type=F32).astype(BF16)
        stacked = jnp.concatenate(
            [absorbed[:, k * block : (k + 1) * block] for k in range(number)], axis=0
        )
        left = projt[:, start * block : (start + number) * block]
        return jnp.dot(left, stacked, preferred_element_type=F32)

    def halo_ready(side):
        def wait():
            for part in range(parts):
                halo_copy(side, part).wait_recv()

        guarded(2 * side - 1, wait)
        if narrow:
            source = jnp.clip(t - 1 + 2 * side, 0, nsec - 1)
            wide_rows = sizes[source] > half

            for j in range(K_NEG // 2):
                piece = halo[side, 0, :, j * block : (j + 1) * block]
                by_row, by_lane = rolled(piece, 0), rolled(piece, 1)
                mixed = jnp.where(wide_rows, by_lane.astype(F32), by_row.astype(F32))
                halo[side, 1, :, j * block : (j + 1) * block] = mixed.astype(BF16)

    def cur_copy(move, dt):
        return pltpu.make_async_remote_copy(
            src_ref=sent.at[move], dst_ref=cur.at[move + 1, 1 - dt],
            send_sem=cur_send.at[move, dt + 1], recv_sem=cur_recv.at[move, 1 - dt],
            device_id={"col": right, "sec": t + dt}, device_id_type=MESH,
        )

    def scale_copy(move, step):
        to = lax.rem(t + step, nsec)
        return pltpu.make_async_remote_copy(
            src_ref=tiles.at[move], dst_ref=scale.at[move, t],
            send_sem=scale_send.at[move, step], recv_sem=scale_recv.at[move, t],
            device_id={"col": right, "sec": to}, device_id_type=MESH,
        )

    def fin_copy(piece):
        return pltpu.make_async_remote_copy(
            src_ref=sent.at[ITERS - 1, piece], dst_ref=fin.at[r],
            send_sem=fin_send.at[piece], recv_sem=fin_recv.at[r],
            device_id={"col": right, "rep": jnp.int32(piece)}, device_id_type=MESH,
        )

    def spread_copy(step, same):
        to = lax.rem(me + step, pair)
        where = {"sec": to // 2, "rep": lax.rem(to, 2)}
        if not same:
            where["col"] = right
        sems, got, dst = (log_send, log_recv, all_last) if same else (next_send, next_recv, last)
        return pltpu.make_async_remote_copy(
            src_ref=last_tile, dst_ref=dst.at[me],
            send_sem=sems.at[step], recv_sem=got.at[me],
            device_id=where, device_id_type=MESH,
        )

    def arrived(ref, sem):
        pltpu.make_async_copy(ref, ref, sem).wait()

    def corner_ready(move, j):
        def wait():
            if move == 0:
                for which in range(2):
                    if j == 1 and which == 0:
                        continue
                    spot_ = cur.at[0, j, r if which == 0 else other]
                    arrived(spot_, first_recv.at[j, which])
            else:
                arrived(cur.at[move, j], cur_recv.at[move - 1, j])

        guarded(j - 1, wait)
        return cur[move, j].reshape(block, block)

    sums = []
    for move in range(ITERS):
        total = part_of(corner_ready(move, 1), own[...], K_NEG)
        for side, j, start in ((0, 0, rise), (1, 2, 0)):
            corner = corner_ready(move, j)
            if move == 0:
                halo_ready(side)
            for part in range(2):
                total = total + part_of(corner, halo[side, part], start + part * K_NEG // 2)
        if move > 0:
            for s in range(nsec):
                arrived(scale.at[move - 1, s], scale_recv.at[move - 1, s])
            whole = jnp.sum(jnp.sum(scale[move - 1], axis=0), keepdims=True)
            total = total / jnp.sqrt(whole / count + 1e-06)
        masked = jnp.where(keep, total, 0.0)
        sent[move] = masked.astype(BF16).reshape(2, half, block)
        if move < ITERS - 1:
            for dt in (1, -1, 0):
                guarded(dt, lambda dt=dt, move=move: cur_copy(move, dt).start())
        else:
            for piece in range(2):
                fin_copy(piece).start()
        squares = jnp.sum((masked * masked).reshape(block // 8, 8, block), axis=0)
        sums.append(jnp.sum(squares, axis=0, keepdims=True))
        if move < ITERS - 1:
            tiles[move] = squares
            for step in range(nsec):
                scale_copy(move, step).start()

    last_tile[...] = jnp.concatenate(sums + [jnp.zeros((8 - ITERS, block), F32)], axis=0)
    for step in range(pair):
        spread_copy(step, False).start()
    for step in range(1, pair):
        spread_copy(step, True).start()
    all_last[me] = last_tile[...]

    for s in range(pair):
        arrived(last.at[s], next_recv.at[s])
    for side in range(2):
        arrived(fin.at[side], fin_recv.at[side])
        whole = last[side]
        for s in range(1, nsec):
            whole = whole + last[2 * s + side]
        whole = jnp.sum(whole[ITERS - 1 : ITERS, :], keepdims=True)
        out[side] = (fin[side].astype(F32) / jnp.sqrt(whole / count + 1e-06)).astype(BF16)

    for step in range(1, pair):
        source = lax.rem(me + step, pair)
        arrived(all_last.at[source], log_recv.at[source])
    diagonal = lax.broadcasted_iota(jnp.int32, (8, block), 0) == lax.broadcasted_iota(
        jnp.int32, (8, block), 1
    )
    for side in range(2):
        whole = all_last[side]
        for s in range(1, nsec):
            whole = whole + all_last[2 * s + side]
        value = jnp.log(jnp.sum(whole, axis=1, keepdims=True) / count + 1e-06)
        row = jnp.sum(jnp.where(diagonal, value, 0.0), axis=0, keepdims=True)
        logs[side : side + 1, :] = row[:, :ITERS]

    send_proj.wait_send()
    for dt, which in firsts:
        guarded(dt, lambda dt=dt, which=which: first_copy(dt, which).wait_send())
    for side in range(2):

        def gone(side=side):
            for part in range(parts):
                halo_copy(side, part).wait_send()

        guarded(1 - 2 * side, gone)
    for move in range(ITERS - 1):
        for dt in (1, -1, 0):
            guarded(dt, lambda dt=dt, move=move: cur_copy(move, dt).wait_send())
        for step in range(nsec):
            scale_copy(move, step).wait_send()
    for piece in range(2):
        fin_copy(piece).wait_send()
    for step in range(pair):
        spread_copy(step, False).wait_send()
    for step in range(1, pair):
        spread_copy(step, True).wait_send()


def on_device(ncol, nsec, corners, edges, projectors, sector_sizes):
    half, block = corners.shape[3:]
    width = edges.shape[4]
    states = width // block
    pair = 2 * nsec
    narrow = 48 * nsec - block - (nsec - 2) <= half
    wide = K_NEG * block // 2
    dma = pltpu.SemaphoreType.DMA
    vmem = pl.BlockSpec(memory_space=pltpu.VMEM)
    anywhere = pl.BlockSpec(memory_space=pl.ANY)
    parked = (2, block, 2 * wide) if narrow else (2, 16, block)
    packed = (2, block, wide) if narrow else (2, 16, block)
    new, logs = pl.pallas_call(
        functools.partial(kernel, ncol, nsec, block, states, narrow),
        out_shape=(
            jax.ShapeDtypeStruct((2, half, block), BF16),
            jax.ShapeDtypeStruct((2, ITERS), F32),
        ),
        in_specs=[pl.BlockSpec(memory_space=pltpu.SMEM), vmem, anywhere, anywhere],
        out_specs=(vmem, vmem),
        scratch_shapes=[
            pltpu.VMEM((block, K_ZERO * block), BF16),
            pltpu.VMEM(parked, BF16),
            pltpu.VMEM(packed, BF16),
            pltpu.VMEM((2, 2, block, wide), BF16),
            pltpu.VMEM((2, half, width), BF16),
            pltpu.VMEM((block, width), BF16),
            pltpu.VMEM((2, half, block), BF16),
            pltpu.VMEM((ITERS, 3, 2, half, block), BF16),
            pltpu.VMEM((ITERS, 2, half, block), BF16),
            pltpu.VMEM((ITERS - 1, nsec, 8, block), F32),
            pltpu.VMEM((ITERS - 1, 8, block), F32),
            pltpu.VMEM((2, half, block), BF16),
            pltpu.VMEM((pair, 8, block), F32),
            pltpu.VMEM((pair, 8, block), F32),
            pltpu.VMEM((8, block), F32),
            dma((4,)),
            dma((2, 2)),
            dma((2, 2)),
            dma,
            dma,
            dma((3, 2)),
            dma((3, 2)),
            dma((ITERS - 1, 3)),
            dma((ITERS - 1, 3)),
            dma((ITERS - 1, nsec)),
            dma((ITERS - 1, nsec)),
            dma((2,)),
            dma((2,)),
            dma((pair,)),
            dma((pair,)),
            dma((pair,)),
            dma((pair,)),
        ],
        compiler_params=pltpu.CompilerParams(
            collective_id=0, has_side_effects=True, vmem_limit_bytes=40 * 2**20
        ),
    )(
        sector_sizes,
        corners.reshape(2, half, block),
        edges.reshape(2, block, width),
        projectors.reshape(2, half, width),
    )
    return new.reshape(corners.shape), logs[None]


def solution(mesh):
    in_specs = (
        P(("grp", "col"), None, "sec", "rep", None),
        P(("grp", "col"), None, "sec", None, None),
        P(("grp", "col"), None, "sec", "rep", None),
        P(),
    )
    out_specs = (P(("grp", "col"), None, "sec", "rep", None), P(("grp", "col"), None, None))
    return jax.shard_map(
        functools.partial(on_device, mesh.shape["col"], mesh.shape["sec"]),
        mesh=mesh, in_specs=in_specs, out_specs=out_specs, check_vma=False,
    )
```

time: 359 us -> 44.8 us (0.12)
  waiting for transfers between devices: 175 us -> 0 us
  blocking collectives: 68.2 us -> 0 us
  Pallas kernels: 0 us -> 38 us
  starting transfers between devices: 35.3 us -> 0 us
  local copies, waits for them, and re-layouts: 39.3 us -> 5.91 us
  matrix products: 18.2 us -> 0 us
  between operations: 14.8 us -> 0.65 us
  other arithmetic: 6.8 us -> 0 us
    ppermute x12 -> x0, waiting for transfers between devices: 95.2 us -> none  [the longest x4 86.1 us: with_halo(): lax.ppermute(lax.slice_in_dim(block, 0, width, axis=dim), axis, backward)]
    unnamed x8 -> x0, waiting for transfers between devices: 79.5 us -> none
    psum x4 -> x0, blocking collectives: 68.2 us -> none  [on_device(): scale = lax.psum(jnp.sum(masked * masked, axis=(1, 2)), ('sec', 'rep'))]
    pallas_call x0 -> x1, Pallas kernels: none -> 38 us  [on_device(): pl.pallas_call(functools.partial(kernel, ncol, nsec, block, states, narro...]
    ppermute x12 -> x0, starting transfers between devices: 35.2 us -> none  [the longest x4 23.9 us: with_halo(): lax.ppermute(lax.slice_in_dim(block, block.shape[dim] - width, None, axis...]
    dot_general x16 -> x0, matrix products: 18.2 us -> none  [the longest x12 10.5 us: project(): jnp.einsum('rakp,rakb->rpb', proj_part, shaped, preferred_element_type=jn...]
    slice x13 -> x0, local copies, waits for them, and re-layouts: 17.6 us -> none  [the longest x4 7.76 us: on_device(): own_part = padded[:, 1, :, K_NEG * block:rise * block]]
    another operation x6 -> x0, local copies, waits for them, and re-layouts: 13.1 us -> none  [the longest x4 8.58 us: project(): shaped = block_part.reshape(2, half, -1, block)]
  transfers between devices with their start and end apart: 16 -> 0, of which waited for: 12 -> 0; matrix products, arithmetic and copies ran while one was open for 10% -> 0% of each run, Pallas kernels for 0% -> 0%
where the time goes in v1:
time: 44.8 us; the launch traced here: 44.6 us
  Pallas kernels  38 us (85%)
  local copies, waits for them, and re-layouts  5.91 us (13%)
  between operations  0.65 us (1%)
    pallas_call x1, Pallas kernels, on_device(): pl.pallas_call(functools.partial(kernel, ncol, nsec, block, states, narro...  38 us
    unnamed x10, local copies, waits for them, and re-layouts  5.91 us

profile of v1, /device:TPU:0, one launch (start us, length us, event | category | flops | bytes accessed | tf_op | source)
XLA Modules:
  0.0 44.6 jit_solution(5942050587766882106)
XLA Ops:
  0.6 0.0 copy-start
  0.6 1.9 %copy-done = bf16[1,2,1,128,6272]{4,3,2,1,0:T(8,128)(2,1)S(1)} copy-done((bf16[1,2,1,128,6272]{4,3,2,1,0:T(8,128)(2,1)S(1)}, bf16[1,2,1,128,6272]{4,3,2,1,0:T(8,128)(2,1)}, u32[]{:S(2)}) %copy-start) | copy-done | bytes 3211288
  2.5 0.0 copy-start.1
  2.5 1.4 %copy-done.1 = bf16[1,2,1,64,6272]{4,3,2,1,0:T(8,128)(2,1)S(1)} copy-done((bf16[1,2,1,64,6272]{4,3,2,1,0:T(8,128)(2,1)S(1)}, bf16[1,2,1,64,6272]{4,3,2,1,0:T(8,128)(2,1)}, u32[]{:S(2)}) %copy-start.1) | copy-done | bytes 1605656
  4.0 0.0 copy-start.2
  4.0 0.8 %copy-done.2 = bf16[1,2,1,64,128]{4,3,2,1,0:T(8,128)(2,1)S(1)} copy-done((bf16[1,2,1,64,128]{4,3,2,1,0:T(8,128)(2,1)S(1)}, bf16[1,2,1,64,128]{4,3,2,1,0:T(8,128)(2,1)}, u32[]{:S(2)}) %copy-start.2) | copy-done | bytes 32792
  4.7 0.0 copy-start.3
  4.7 0.7 %copy-done.3 = s32[4]{0:T(128)S(1)} copy-done((s32[4]{0:T(128)S(1)}, s32[4]{0:T(128)}, u32[]{:S(2)}) %copy-start.3) | copy-done | bytes 40
  5.4 38.0 %shard_map.59 = (bf16[2,64,128]{2,1,0:T(8,128)(2,1)S(1)}, f32[2,4]{1,0:T(2,128)S(1)}) custom-call(s32[4]{0:T(128)S(1)} %copy-done.3, bf16[2,64,128]{2,1,0:T(8,128)(2,1)S(1)} %bitcast.9, bf16[2,128,6272]{2,1,0:T(8,128)(2,1)S(1)} %bitcast.7, bf16[2,64,6272]{2,1,0:T(8,128)(2,1)S(1)} %bitcast.8), custom_call_target="tpu_custom_call" | custom-call | tf_op jit(solution)/shard_map/pallas_call | solution.py:331
  43.4 0.6 %copy.9 = bf16[1,2,1,64,128]{4,3,2,1,0:T(8,128)(2,1)} copy(bf16[1,2,1,64,128]{4,3,2,1,0:T(8,128)(2,1)S(1)} %bitcast.10) | data formatting | bytes 65536
  44.0 0.6 %copy.10 = f32[1,2,4]{2,1,0:T(2,128)} copy(f32[1,2,4]{2,1,0:T(2,128)S(1)} %bitcast.11) | data formatting | bytes 64
Async XLA Ops:
  0.6 1.9 %copy-start = (bf16[1,2,1,128,6272]{4,3,2,1,0:T(8,128)(2,1)S(1)}, bf16[1,2,1,128,6272]{4,3,2,1,0:T(8,128)(2,1)}, u32[]{:S(2)}) copy-start(bf16[1,2,1,128,6272]{4,3,2,1,0:T(8,128)(2,1)} %param.5) | copy-start | bytes 9633796
  2.5 1.4 %copy-start.1 = (bf16[1,2,1,64,6272]{4,3,2,1,0:T(8,128)(2,1)S(1)}, bf16[1,2,1,64,6272]{4,3,2,1,0:T(8,128)(2,1)}, u32[]{:S(2)}) copy-start(bf16[1,2,1,64,6272]{4,3,2,1,0:T(8,128)(2,1)} %param.6) | copy-start | bytes 4816900
  4.0 0.8 %copy-start.2 = (bf16[1,2,1,64,128]{4,3,2,1,0:T(8,128)(2,1)S(1)}, bf16[1,2,1,64,128]{4,3,2,1,0:T(8,128)(2,1)}, u32[]{:S(2)}) copy-start(bf16[1,2,1,64,128]{4,3,2,1,0:T(8,128)(2,1)} %param.4) | copy-start | bytes 98308
  4.7 0.7 %copy-start.3 = (s32[4]{0:T(128)S(1)}, s32[4]{0:T(128)}, u32[]{:S(2)}) copy-start(s32[4]{0:T(128)} %sizes.1) | copy-start | bytes 52

commit v2 on v1

--- a/solution.py
+++ b/solution.py
@@ -24,9 +24,9 @@
 
 def kernel(
     ncol, nsec, block, states, narrow,
-    sizes, corners, edges, projectors,
+    sizes_in, corners_in, edges, projectors,
     out, logs,
-    own, stage, packed, halo, proj, projt, first, cur, sent, scale, tiles, fin, last, all_last, last_tile,
+    sizes, corners, own, stage, packed, halo, proj, projt, first, cur, sent, scale, tiles, fin, last, all_last, last_tile,
     load_sem, halo_send, halo_recv, proj_send, proj_recv, first_send, first_recv,
     cur_send, cur_recv, scale_send, scale_recv, fin_send, fin_recv, next_send, next_recv, log_send, log_recv,
 ):
@@ -49,7 +49,9 @@
             pltpu.make_async_copy(edges.at[r, :, rise * block :], stage.at[0], load_sem.at[2]),
             pltpu.make_async_copy(edges.at[r, :, : K_NEG * block], stage.at[1], load_sem.at[3]),
         ]
-    for copy in loads + [load_proj, load_own]:
+    load_sizes = pltpu.make_async_copy(sizes_in, sizes, load_sem.at[4])
+    load_corners = pltpu.make_async_copy(corners_in, corners, load_sem.at[5])
+    for copy in [load_sizes, load_corners] + loads + [load_proj, load_own]:
         copy.start()
 
     barrier = pltpu.get_barrier_semaphore()
@@ -65,6 +67,7 @@
             device_id_type=MESH,
         )
 
+    load_sizes.wait()
     live = sizes[t]
     count = jnp.float32(0.0)
     for s in range(nsec):
@@ -76,6 +79,7 @@
     half_rows = lax.broadcasted_iota(jnp.int32, (half, block), 0) + r * half
     half_lanes = lax.broadcasted_iota(jnp.int32, (half, block), 1)
     half_keep = (half_rows < live) & (half_lanes < live)
+    load_corners.wait()
     for which in range(2):
         value = corners[which].astype(F32)
         first[which] = jnp.where(half_keep, value, 0.0).astype(BF16)
@@ -89,6 +93,16 @@
     def _():
         cur[:, 2] = jnp.zeros((ITERS, 2, half, block), BF16)
         halo[1] = jnp.zeros((2, block, wide), BF16)
+
+    for side in range(len(loads)):
+        loads[side].wait()
+        for j in range(K_NEG // 2):
+            low = stage[side, :, j * block : (j + 1) * block]
+            high = stage[side, :, wide + j * block : wide + (j + 1) * block]
+            by_row = jnp.concatenate([low[:half], high[:half]], axis=0)
+            by_lane = jnp.concatenate([low[:, :half], high[:, :half]], axis=1)
+            mixed = jnp.where(live > half, by_lane.astype(F32), by_row.astype(F32))
+            packed[side, :, j * block : (j + 1) * block] = mixed.astype(BF16)
 
     pl.semaphore_wait(barrier, everyone - 1)
 
@@ -99,26 +113,6 @@
             action()
         else:
             pl.when(has_high if dt > 0 else has_low)(action)
-
-    send_proj = pltpu.make_async_remote_copy(
-        src_ref=projectors.at[other], dst_ref=proj.at[r],
-        send_sem=proj_send, recv_sem=proj_recv,
-        device_id={"rep": other}, device_id_type=MESH,
-    )
-    send_proj.start()
-
-    def first_copy(dt, which):
-        side = r if which == 0 else other
-        return pltpu.make_async_remote_copy(
-            src_ref=first.at[side], dst_ref=cur.at[0, 1 - dt, r],
-            send_sem=first_send.at[dt + 1, which], recv_sem=first_recv.at[1 - dt, which],
-            device_id={"sec": t + dt, "rep": side}, device_id_type=MESH,
-        )
-
-    firsts = [(0, 1), (1, 0), (1, 1), (-1, 0), (-1, 1)]
-    for dt, which in firsts:
-        guarded(dt, lambda dt=dt, which=which: first_copy(dt, which).start())
-    cur[0, 1, r] = first[r]
 
     def halo_copy(side, part):
         if narrow:
@@ -134,21 +128,32 @@
 
     parts = 1 if narrow else 2
     for side in range(2):
-        if narrow:
-            loads[side].wait()
-            for j in range(K_NEG // 2):
-                low = stage[side, :, j * block : (j + 1) * block]
-                high = stage[side, :, wide + j * block : wide + (j + 1) * block]
-                by_row = jnp.concatenate([low[:half], high[:half]], axis=0)
-                by_lane = jnp.concatenate([low[:, :half], high[:, :half]], axis=1)
-                mixed = jnp.where(live > half, by_lane.astype(F32), by_row.astype(F32))
-                packed[side, :, j * block : (j + 1) * block] = mixed.astype(BF16)
 
         def go(side=side):
             for part in range(parts):
                 halo_copy(side, part).start()
 
         guarded(1 - 2 * side, go)
+
+    send_proj = pltpu.make_async_remote_copy(
+        src_ref=projectors.at[other], dst_ref=proj.at[r],
+        send_sem=proj_send, recv_sem=proj_recv,
+        device_id={"rep": other}, device_id_type=MESH,
+    )
+    send_proj.start()
+
+    def first_copy(dt, which):
+        side = r if which == 0 else other
+        return pltpu.make_async_remote_copy(
+            src_ref=first.at[side], dst_ref=cur.at[0, 1 - dt, r],
+            send_sem=first_send.at[dt + 1, which], recv_sem=first_recv.at[1 - dt, which],
+            device_id={"sec": t + dt, "rep": side}, device_id_type=MESH,
+        )
+
+    firsts = [(0, 1), (1, 0), (1, 1), (-1, 0), (-1, 1)]
+    for dt, which in firsts:
+        guarded(dt, lambda dt=dt, which=which: first_copy(dt, which).start())
+    cur[0, 1, r] = first[r]
 
     load_proj.wait()
     send_proj.wait_recv()
@@ -250,7 +255,7 @@
         masked = jnp.where(keep, total, 0.0)
         sent[move] = masked.astype(BF16).reshape(2, half, block)
         if move < ITERS - 1:
-            for dt in (1, -1, 0):
+            for dt in (0, 1, -1):
                 guarded(dt, lambda dt=dt, move=move: cur_copy(move, dt).start())
         else:
             for piece in range(2):
@@ -334,9 +339,11 @@
             jax.ShapeDtypeStruct((2, half, block), BF16),
             jax.ShapeDtypeStruct((2, ITERS), F32),
         ),
-        in_specs=[pl.BlockSpec(memory_space=pltpu.SMEM), vmem, anywhere, anywhere],
+        in_specs=[anywhere] * 4,
         out_specs=(vmem, vmem),
         scratch_shapes=[
+            pltpu.SMEM((nsec,), jnp.int32),
+            pltpu.VMEM((2, half, block), BF16),
             pltpu.VMEM((block, K_ZERO * block), BF16),
             pltpu.VMEM(parked, BF16),
             pltpu.VMEM(packed, BF16),
@@ -352,7 +359,7 @@
             pltpu.VMEM((pair, 8, block), F32),
             pltpu.VMEM((pair, 8, block), F32),
             pltpu.VMEM((8, block), F32),
-            dma((4,)),
+            dma((6,)),
             dma((2, 2)),
             dma((2, 2)),
             dma,
@@ -371,7 +378,7 @@
             dma((pair,)),
         ],
         compiler_params=pltpu.CompilerParams(
-            collective_id=0, has_side_effects=True, vmem_limit_bytes=40 * 2**20
+            collective_id=0, has_side_effects=True, vmem_limit_bytes=60 * 2**20
         ),
     )(
         sector_sizes,

time: 44.8 us -> 41.6 us (0.929)
  local copies, waits for them, and re-layouts: 5.91 us -> 2.6 us
    unnamed x10 -> x2, local copies, waits for them, and re-layouts: 5.91 us -> 2.6 us
where the time goes in v2:
time: 41.6 us; the launch traced here: 41.4 us
  Pallas kernels  38.2 us (92%)
  local copies, waits for them, and re-layouts  2.6 us (6%)
  between operations  0.64 us (2%)
    pallas_call x1, Pallas kernels, on_device(): pl.pallas_call(functools.partial(kernel, ncol, nsec, block, states, narro...  38.2 us
    unnamed x2, local copies, waits for them, and re-layouts  2.6 us

profile of v2, /device:TPU:0, one launch (start us, length us, event | category | flops | bytes accessed | tf_op | source)
XLA Modules:
  0.0 41.4 jit_solution(10222164707935898649)
XLA Ops:
  0.6 38.2 %shard_map.59 = (bf16[2,64,128]{2,1,0:T(8,128)(2,1)}, f32[2,4]{1,0:T(2,128)}) custom-call(s32[4]{0:T(128)} %sizes_in.1, bf16[2,64,128]{2,1,0:T(8,128)(2,1)} %bitcast.9, bf16[2,128,6272]{2,1,0:T(8,128)(2,1)} %bitcast.7, bf16[2,64,6272]{2,1,0:T(8,128)(2,1)} %bitcast.8), custom_call_target="tpu_custom_call" | custom-call | tf_op jit(solution)/shard_map/pallas_call | solution.py:336
  38.8 1.4 %copy.9 = bf16[1,2,1,64,128]{4,3,2,1,0:T(8,128)(2,1)} copy(bf16[1,2,1,64,128]{4,3,2,1,0:T(8,128)(2,1)} %bitcast.10) | data formatting | bytes 65536
  40.2 1.2 %copy.10 = f32[1,2,4]{2,1,0:T(2,128)} copy(f32[1,2,4]{2,1,0:T(2,128)} %bitcast.11) | data formatting | bytes 64

commit v3 on v2

--- a/solution.py
+++ b/solution.py
@@ -28,11 +28,12 @@
     out, logs,
     sizes, corners, own, stage, packed, halo, proj, projt, first, cur, sent, scale, tiles, fin, last, all_last, last_tile,
     load_sem, halo_send, halo_recv, proj_send, proj_recv, first_send, first_recv,
-    cur_send, cur_recv, scale_send, scale_recv, fin_send, fin_recv, next_send, next_recv, log_send, log_recv,
+    cur_send, cur_recv, scale_send, scale_recv, fin_send, fin_recv, next_send, next_recv, log_send, log_recv, word,
 ):
     half = block // 2
     rise = K_NEG + K_ZERO
     wide = K_NEG * block // 2
+    piece_wide = wide // 2
     c, t, r = lax.axis_index("col"), lax.axis_index("sec"), lax.axis_index("rep")
     other = 1 - r
     right = lax.rem(c + 1, ncol)
@@ -54,18 +55,31 @@
     for copy in [load_sizes, load_corners] + loads + [load_proj, load_own]:
         copy.start()
 
+    has_low, has_high = t > 0, t < nsec - 1
+
+    def guarded(dt, action):
+        if dt == 0:
+            action()
+        else:
+            pl.when(has_high if dt > 0 else has_low)(action)
+
     barrier = pltpu.get_barrier_semaphore()
-    everyone = ncol * pair
-    spot = c * pair + me
-
-    @pl.loop(1, everyone)
-    def _(step):
-        to = lax.rem(spot + step, everyone)
-        pl.semaphore_signal(
-            barrier, inc=1,
-            device_id={"col": to // pair, "sec": lax.rem(to, pair) // 2, "rep": lax.rem(to, 2)},
-            device_id_type=MESH,
-        )
+
+    def greet(where):
+        pl.semaphore_signal(barrier, inc=1, device_id=where, device_id_type=MESH)
+
+    columns = [right] if ncol == 2 else [right, lax.rem(c + ncol - 1, ncol)]
+    greet({"rep": other})
+    for column in columns:
+        greet({"col": column})
+        greet({"col": column, "rep": other})
+    for dt in (1, -1):
+
+        def greet_sector(dt=dt):
+            greet({"sec": t + dt})
+            greet({"sec": t + dt, "rep": other})
+
+        guarded(dt, greet_sector)
 
     load_sizes.wait()
     live = sizes[t]
@@ -87,12 +101,12 @@
     @pl.when(t == 0)
     def _():
         cur[:, 0] = jnp.zeros((ITERS, 2, half, block), BF16)
-        halo[0] = jnp.zeros((2, block, wide), BF16)
+        halo[0] = jnp.zeros((block, 2 * wide), BF16)
 
     @pl.when(t == nsec - 1)
     def _():
         cur[:, 2] = jnp.zeros((ITERS, 2, half, block), BF16)
-        halo[1] = jnp.zeros((2, block, wide), BF16)
+        halo[1] = jnp.zeros((block, 2 * wide), BF16)
 
     for side in range(len(loads)):
         loads[side].wait()
@@ -102,38 +116,42 @@
             by_row = jnp.concatenate([low[:half], high[:half]], axis=0)
             by_lane = jnp.concatenate([low[:, :half], high[:, :half]], axis=1)
             mixed = jnp.where(live > half, by_lane.astype(F32), by_row.astype(F32))
-            packed[side, :, j * block : (j + 1) * block] = mixed.astype(BF16)
-
-    pl.semaphore_wait(barrier, everyone - 1)
-
-    has_low, has_high = t > 0, t < nsec - 1
-
-    def guarded(dt, action):
-        if dt == 0:
-            action()
+            place = slice(j % 4 * block, (j % 4 + 1) * block)
+            packed[side, j // 4, :, place] = mixed.astype(BF16)
+
+    lower = (t + nsec - 2) // (nsec - 1)
+    upper = (2 * nsec - 3 - t) // (nsec - 1)
+    pl.semaphore_wait(barrier, 1 + 2 * len(columns) + 2 * lower + 2 * upper)
+
+    def pass_on(dt):
+        pl.semaphore_signal(
+            word.at[(dt + 1) // 2], inc=1, device_id={"sec": t + dt}, device_id_type=MESH
+        )
+
+    pl.when(t == 0)(lambda: pass_on(1))
+    pl.when(t == nsec - 1)(lambda: pass_on(-1))
+
+    def halo_copy(side, chunk, part):
+        if narrow:
+            src = packed.at[side, chunk]
         else:
-            pl.when(has_high if dt > 0 else has_low)(action)
-
-    def halo_copy(side, part):
-        if narrow:
-            src = packed.at[side]
-        else:
-            start = (rise * block if side == 0 else 0) + part * wide
-            src = edges.at[r, :, start : start + wide]
-        return pltpu.make_async_remote_copy(
-            src_ref=src, dst_ref=halo.at[side, part],
-            send_sem=halo_send.at[side, part], recv_sem=halo_recv.at[side, part],
+            start = (rise * block if side == 0 else 0) + part * wide + chunk * piece_wide
+            src = edges.at[r, :, start : start + piece_wide]
+        return pltpu.make_async_remote_copy(
+            src_ref=src, dst_ref=halo.at[side, :, part * wide + chunk * piece_wide : part * wide + (chunk + 1) * piece_wide],
+            send_sem=halo_send.at[side, chunk, part], recv_sem=halo_recv.at[side, chunk, part],
             device_id={"sec": t + 1 - 2 * side}, device_id_type=MESH,
         )
 
     parts = 1 if narrow else 2
-    for side in range(2):
-
-        def go(side=side):
-            for part in range(parts):
-                halo_copy(side, part).start()
-
-        guarded(1 - 2 * side, go)
+    for chunk in range(2):
+        for side in range(2):
+
+            def go(side=side, chunk=chunk):
+                for part in range(parts):
+                    halo_copy(side, chunk, part).start()
+
+            guarded(1 - 2 * side, go)
 
     send_proj = pltpu.make_async_remote_copy(
         src_ref=projectors.at[other], dst_ref=proj.at[r],
@@ -162,6 +180,11 @@
         projt[:, k * block : (k + 1) * block] = piece.T
     load_own.wait()
 
+    between = jnp.logical_and(has_low, has_high)
+    for dt in (1, -1):
+        guarded(-dt, lambda dt=dt: pl.semaphore_wait(word.at[(dt + 1) // 2], 1))
+        pl.when(between)(lambda dt=dt: pass_on(dt))
+
     def part_of(corner, edge, start):
         number = edge.shape[1] // block
         absorbed = jnp.dot(corner, edge, preferred_element_type=F32).astype(BF16)
@@ -171,21 +194,21 @@
         left = projt[:, start * block : (start + number) * block]
         return jnp.dot(left, stacked, preferred_element_type=F32)
 
-    def halo_ready(side):
+    def halo_ready(side, chunk):
         def wait():
             for part in range(parts):
-                halo_copy(side, part).wait_recv()
+                halo_copy(side, chunk, part).wait_recv()
 
         guarded(2 * side - 1, wait)
         if narrow:
             source = jnp.clip(t - 1 + 2 * side, 0, nsec - 1)
             wide_rows = sizes[source] > half
 
-            for j in range(K_NEG // 2):
-                piece = halo[side, 0, :, j * block : (j + 1) * block]
+            for j in range(K_NEG // 4 * chunk, K_NEG // 4 * (chunk + 1)):
+                piece = halo[side, :, j * block : (j + 1) * block]
                 by_row, by_lane = rolled(piece, 0), rolled(piece, 1)
                 mixed = jnp.where(wide_rows, by_lane.astype(F32), by_row.astype(F32))
-                halo[side, 1, :, j * block : (j + 1) * block] = mixed.astype(BF16)
+                halo[side, :, wide + j * block : wide + (j + 1) * block] = mixed.astype(BF16)
 
     def cur_copy(move, dt):
         return pltpu.make_async_remote_copy(
@@ -244,22 +267,19 @@
         for side, j, start in ((0, 0, rise), (1, 2, 0)):
             corner = corner_ready(move, j)
             if move == 0:
-                halo_ready(side)
-            for part in range(2):
-                total = total + part_of(corner, halo[side, part], start + part * K_NEG // 2)
+                for chunk in range(2):
+                    halo_ready(side, chunk)
+            total = total + part_of(corner, halo[side], start)
         if move > 0:
             for s in range(nsec):
                 arrived(scale.at[move - 1, s], scale_recv.at[move - 1, s])
             whole = jnp.sum(jnp.sum(scale[move - 1], axis=0), keepdims=True)
             total = total / jnp.sqrt(whole / count + 1e-06)
         masked = jnp.where(keep, total, 0.0)
-        sent[move] = masked.astype(BF16).reshape(2, half, block)
         if move < ITERS - 1:
+            sent[move] = masked.astype(BF16).reshape(2, half, block)
             for dt in (0, 1, -1):
                 guarded(dt, lambda dt=dt, move=move: cur_copy(move, dt).start())
-        else:
-            for piece in range(2):
-                fin_copy(piece).start()
         squares = jnp.sum((masked * masked).reshape(block // 8, 8, block), axis=0)
         sums.append(jnp.sum(squares, axis=0, keepdims=True))
         if move < ITERS - 1:
@@ -268,8 +288,11 @@
                 scale_copy(move, step).start()
 
     last_tile[...] = jnp.concatenate(sums + [jnp.zeros((8 - ITERS, block), F32)], axis=0)
-    for step in range(pair):
+    for step in range(pair - 1, -1, -1):
         spread_copy(step, False).start()
+    sent[ITERS - 1] = masked.astype(BF16).reshape(2, half, block)
+    for piece in range(2):
+        fin_copy(piece).start()
     for step in range(1, pair):
         spread_copy(step, True).start()
     all_last[me] = last_tile[...]
@@ -304,8 +327,9 @@
     for side in range(2):
 
         def gone(side=side):
-            for part in range(parts):
-                halo_copy(side, part).wait_send()
+            for chunk in range(2):
+                for part in range(parts):
+                    halo_copy(side, chunk, part).wait_send()
 
         guarded(1 - 2 * side, gone)
     for move in range(ITERS - 1):
@@ -332,7 +356,7 @@
     vmem = pl.BlockSpec(memory_space=pltpu.VMEM)
     anywhere = pl.BlockSpec(memory_space=pl.ANY)
     parked = (2, block, 2 * wide) if narrow else (2, 16, block)
-    packed = (2, block, wide) if narrow else (2, 16, block)
+    packed = (2, 2, block, wide // 2) if narrow else (2, 2, 16, block)
     new, logs = pl.pallas_call(
         functools.partial(kernel, ncol, nsec, block, states, narrow),
         out_shape=(
@@ -347,7 +371,7 @@
             pltpu.VMEM((block, K_ZERO * block), BF16),
             pltpu.VMEM(parked, BF16),
             pltpu.VMEM(packed, BF16),
-            pltpu.VMEM((2, 2, block, wide), BF16),
+            pltpu.VMEM((2, block, 2 * wide), BF16),
             pltpu.VMEM((2, half, width), BF16),
             pltpu.VMEM((block, width), BF16),
             pltpu.VMEM((2, half, block), BF16),
@@ -360,8 +384,8 @@
             pltpu.VMEM((pair, 8, block), F32),
             pltpu.VMEM((8, block), F32),
             dma((6,)),
-            dma((2, 2)),
-            dma((2, 2)),
+            dma((2, 2, 2)),
+            dma((2, 2, 2)),
             dma,
             dma,
             dma((3, 2)),
@@ -376,6 +400,7 @@
             dma((pair,)),
             dma((pair,)),
             dma((pair,)),
+            pltpu.SemaphoreType.REGULAR((2,)),
         ],
         compiler_params=pltpu.CompilerParams(
             collective_id=0, has_side_effects=True, vmem_limit_bytes=60 * 2**20

time: 41.6 us -> 39.3 us (0.945)
  Pallas kernels: 38.2 us -> 35.8 us
    pallas_call x1, Pallas kernels: 38.2 us -> 35.8 us  [on_device(): pl.pallas_call(functools.partial(kernel, ncol, nsec, block, states, narro...]
where the time goes in v3:
time: 39.3 us; the launch traced here: 39.1 us
  Pallas kernels  35.8 us (91%)
  local copies, waits for them, and re-layouts  2.6 us (7%)
  between operations  0.64 us (2%)
    pallas_call x1, Pallas kernels, on_device(): pl.pallas_call(functools.partial(kernel, ncol, nsec, block, states, narro...  35.8 us
    unnamed x2, local copies, waits for them, and re-layouts  2.6 us

profile of v3, /device:TPU:0, one launch (start us, length us, event | category | flops | bytes accessed | tf_op | source)
XLA Modules:
  0.0 39.1 jit_solution(7925939470128248447)
XLA Ops:
  0.6 35.8 %shard_map.59 = (bf16[2,64,128]{2,1,0:T(8,128)(2,1)}, f32[2,4]{1,0:T(2,128)}) custom-call(s32[4]{0:T(128)} %sizes_in.1, bf16[2,64,128]{2,1,0:T(8,128)(2,1)} %bitcast.9, bf16[2,128,6272]{2,1,0:T(8,128)(2,1)} %bitcast.7, bf16[2,64,6272]{2,1,0:T(8,128)(2,1)} %bitcast.8), custom_call_target="tpu_custom_call" | custom-call | tf_op jit(solution)/shard_map/pallas_call | solution.py:360
  36.5 1.4 %copy.9 = bf16[1,2,1,64,128]{4,3,2,1,0:T(8,128)(2,1)} copy(bf16[1,2,1,64,128]{4,3,2,1,0:T(8,128)(2,1)} %bitcast.10) | data formatting | bytes 65536
  37.8 1.2 %copy.10 = f32[1,2,4]{2,1,0:T(2,128)} copy(f32[1,2,4]{2,1,0:T(2,128)} %bitcast.11) | data formatting | bytes 64

commit v4 on v3

--- a/solution.py
+++ b/solution.py
@@ -177,7 +177,8 @@
     send_proj.wait_recv()
     for k in range(states):
         piece = proj[:, :, k * block : (k + 1) * block].reshape(block, block)
-        projt[:, k * block : (k + 1) * block] = piece.T
+        place = k - rise if k >= rise else k + K_NEG
+        projt[:, place * block : (place + 1) * block] = piece.T
     load_own.wait()
 
     between = jnp.logical_and(has_low, has_high)
@@ -185,13 +186,13 @@
         guarded(-dt, lambda dt=dt: pl.semaphore_wait(word.at[(dt + 1) // 2], 1))
         pl.when(between)(lambda dt=dt: pass_on(dt))
 
-    def part_of(corner, edge, start):
-        number = edge.shape[1] // block
+    def absorb(corner, edge):
         absorbed = jnp.dot(corner, edge, preferred_element_type=F32).astype(BF16)
-        stacked = jnp.concatenate(
-            [absorbed[:, k * block : (k + 1) * block] for k in range(number)], axis=0
-        )
-        left = projt[:, start * block : (start + number) * block]
+        return [absorbed[:, k : k + block] for k in range(0, edge.shape[1], block)]
+
+    def project(pieces, start):
+        stacked = jnp.concatenate(pieces, axis=0)
+        left = projt[:, start * block : (start + len(pieces)) * block]
         return jnp.dot(left, stacked, preferred_element_type=F32)
 
     def halo_ready(side, chunk):
@@ -263,13 +264,15 @@
 
     sums = []
     for move in range(ITERS):
-        total = part_of(corner_ready(move, 1), own[...], K_NEG)
-        for side, j, start in ((0, 0, rise), (1, 2, 0)):
+        total = project(absorb(corner_ready(move, 1), own[...]), 2 * K_NEG)
+        around = []
+        for side, j in ((0, 0), (1, 2)):
             corner = corner_ready(move, j)
             if move == 0:
                 for chunk in range(2):
                     halo_ready(side, chunk)
-            total = total + part_of(corner, halo[side], start)
+            around = around + absorb(corner, halo[side])
+        total = total + project(around, 0)
         if move > 0:
             for s in range(nsec):
                 arrived(scale.at[move - 1, s], scale_recv.at[move - 1, s])
@@ -411,6 +414,27 @@
         edges.reshape(2, block, width),
         projectors.reshape(2, half, width),
     )
+    def write(new_ref, logs_ref, new_out, logs_out, sems):
+        copies = [
+            pltpu.make_async_copy(new_ref, new_out, sems.at[0]),
+            pltpu.make_async_copy(logs_ref, logs_out, sems.at[1]),
+        ]
+        for copy in copies:
+            copy.start()
+        for copy in copies:
+            copy.wait()
+
+    new, logs = pl.pallas_call(
+        write,
+        out_shape=(
+            jax.ShapeDtypeStruct((2, half, block), BF16),
+            jax.ShapeDtypeStruct((2, ITERS), F32),
+        ),
+        in_specs=[anywhere, anywhere],
+        out_specs=(anywhere, anywhere),
+        scratch_shapes=[dma((2,))],
+        compiler_params=pltpu.CompilerParams(vmem_limit_bytes=60 * 2**20),
+    )(new, logs)
     return new.reshape(corners.shape), logs[None]
 
 

time: 39.3 us -> 38.5 us (0.980)
  local copies, waits for them, and re-layouts: 2.6 us -> 0 us
  Pallas kernels: 35.8 us -> 37.7 us
    unnamed x2 -> x0, local copies, waits for them, and re-layouts: 2.6 us -> none
    pallas_call x0 -> x1, Pallas kernels: none -> 2.14 us  [on_device(): pl.pallas_call(write, out_shape=(jax.ShapeDtypeStruct((2, half, block), B...]
where the time goes in v4:
time: 38.5 us; the launch traced here: 38.4 us
  Pallas kernels  37.7 us (98%)
  between operations  0.64 us (2%)
    pallas_call x1, Pallas kernels, on_device(): pl.pallas_call(functools.partial(kernel, ncol, nsec, block, states, narro...  35.6 us
    pallas_call x1, Pallas kernels, on_device(): pl.pallas_call(write, out_shape=(jax.ShapeDtypeStruct((2, half, block), B...  2.14 us

profile of v4, /device:TPU:0, one launch (start us, length us, event | category | flops | bytes accessed | tf_op | source)
XLA Modules:
  0.0 38.4 jit_solution(7703175664595332016)
XLA Ops:
  0.6 35.6 %shard_map.59 = (bf16[2,64,128]{2,1,0:T(8,128)(2,1)}, f32[2,4]{1,0:T(2,128)}) custom-call(s32[4]{0:T(128)} %sizes_in.1, bf16[2,64,128]{2,1,0:T(8,128)(2,1)} %bitcast.9, bf16[2,128,6272]{2,1,0:T(8,128)(2,1)} %bitcast.7, bf16[2,64,6272]{2,1,0:T(8,128)(2,1)} %bitcast.8), custom_call_target="tpu_custom_call" | custom-call | tf_op jit(solution)/shard_map/pallas_call | solution.py:363
  36.2 2.1 %shard_map.60 = (bf16[2,64,128]{2,1,0:T(8,128)(2,1)}, f32[2,4]{1,0:T(2,128)}) custom-call(bf16[2,64,128]{2,1,0:T(8,128)(2,1)} %get-tuple-element.6.new_ref, f32[2,4]{1,0:T(2,128)} %get-tuple-element.7.logs_ref), custom_call_target="tpu_custom_call" | custom-call | tf_op jit(solution)/shard_map/pallas_call | solution.py:427
